TPU v7x, 512 devices: a whole 4x4x16 slice. The times are simulated.
512 devices in a mesh: dp: 32 (over y, z_lo, core), shard: 16 (over z_hi, x).
Axes of the slice: x: 4, y: 4, z: 16 (z_hi: 4, z_lo: 4; z = z_hi * 4 + z_lo), core: 2. Of those that a mesh axis runs over, the one named last changes fastest.
Arguments:
- layer_input: bfloat16 [16384, 8192], P('dp', 'shard'), may hold values from -6 to 6
- out_grad: bfloat16 [16384, 14336], P('dp', 'shard'), may hold values from -48 to 48
- projector: bfloat16 [8192, 1024], P(('dp', 'shard')), may hold values from -0.0625 to 0.0625
- first_moment: float32 [1024, 14336], P('dp', 'shard'), may hold values from -1.75 to 1.75
- second_moment: float32 [1024, 14336], P('dp', 'shard'), may hold values from 0.05 to 0.5
- doc_ids: int32 [16384], P('dp'), may hold values from 0 to 31, as said below
Outputs:
- new_first: float32 [1024, 14336], P('dp', 'shard')
- new_second: float32 [1024, 14336], P('dp', 'shard')
- update: bfloat16 [8192, 14336], P('dp', 'shard')
Inputs may be any that keep to these rules, and one draw needn't show every extreme that they name: `doc_ids`: numbers never fall along the tokens; every number from 0 to 31 occurs, each on 256 tokens or more.
All inputs are finite; a program needn't handle non-finite values.
Results may differ from a plain program's by a relative error of at most 0.0055.
Values may be sent and summed in bfloat16 or wider, within the bound.
A program may use at most 64 MiB of HBM per device.

v0:
```python
import jax
import jax.numpy as jnp
from jax import lax
from jax.sharding import PartitionSpec as P

beta_first = 0.9
beta_second = 0.95
bias_first = 1.0 - beta_first**2
bias_second = 1.0 - beta_second**2
epsilon = 1e-08


def broadcast(block, axis, holder):
    block = jnp.where(lax.axis_index(axis) == holder, block, jnp.zeros_like(block))
    return lax.psum(block, axis)


def adam_step(first_moment, second_moment, gradient):
    new_first = beta_first * first_moment + (1.0 - beta_first) * gradient
    new_second = beta_second * second_moment + (1.0 - beta_second) * (gradient * gradient)
    direction = (new_first / bias_first / (jnp.sqrt(new_second / bias_second) + epsilon)).astype(
        jnp.bfloat16
    )
    return (new_first, new_second, direction)


def local(layer_input, out_grad, projector, first_moment, second_moment, doc_ids):
    dp_count = lax.axis_size("dp")
    shard_count = lax.axis_size("shard")
    shard_index = lax.axis_index("shard")
    doc_match = (doc_ids[:, None] == jnp.arange(dp_count, dtype=jnp.int32)[None, :]).astype(
        jnp.float32
    )
    lengths = lax.psum(jnp.sum(doc_match, axis=0), "dp")
    token_weight = jnp.sum(doc_match * (1.0 / lengths)[None, :], axis=1)
    block_rows = lax.all_gather(projector, "shard", axis=0, tiled=True)
    block_ratio = dp_count // shard_count
    portions = []
    for member in range(block_ratio):
        portions.append(broadcast(block_rows, "dp", block_ratio * shard_index + member))
    input_rows = jnp.concatenate(portions, axis=0)
    partial_value = jnp.dot(layer_input, input_rows, preferred_element_type=jnp.float32)
    projected = lax.psum(partial_value, "shard")
    weighted = (projected * token_weight[:, None]).astype(jnp.bfloat16)
    contract = (((0,), (0,)), ((), ()))
    gradient = lax.psum_scatter(
        lax.dot_general(weighted, out_grad, contract, preferred_element_type=jnp.float32),
        "dp",
        scatter_dimension=0,
        tiled=True,
    )
    new_first, new_second, direction = adam_step(first_moment, second_moment, gradient)
    update = jnp.dot(
        block_rows,
        lax.all_gather(direction, "dp", axis=0, tiled=True),
        preferred_element_type=jnp.float32,
    )
    return (new_first, new_second, update.astype(jnp.bfloat16))


def solution(mesh):
    placed = (
        P("dp", "shard"),
        P("dp", "shard"),
        P(("dp", "shard"), None),
        P("dp", "shard"),
        P("dp", "shard"),
        P("dp"),
    )
    return jax.shard_map(
        local,
        mesh=mesh,
        in_specs=placed,
        out_specs=(P("dp", "shard"), P("dp", "shard"), P("dp", "shard")),
        check_vma=False,
    )
```

profile of v0, /device:TPU:1, one launch (start us, length us, event | category | flops | bytes accessed | tf_op | source)
XLA Modules:
  0.0 851.4 jit_solution(1585809910006604408)
XLA Ops:
  7.2 0.0 copy-start
  7.2 0.0 copy-start.1
  7.2 0.0 all-reduce.6.cloned.1.call-start
  7.2 56.7 %all_gather.6 = bf16[256,1024]{1,0:T(8,128)(2,1)S(1)} all-gather(bf16[16,1024]{1,0:T(8,128)(2,1)} %param.8), channel_id=1, replica_groups=mesh['dp'=32,'shard'=16] {'shard'}, dimensions={0}, use_global_device_ids=true | all-gather | bytes 557056 | tf_op jit(solution)/shard_map/all_gather | solution.py:36
  63.9 1.0 broadcast_select_fusion.1
  65.0 0.0 all-reduce.6.cloned.1.call-update
  65.0 0.0 all-reduce.4.cloned.1.call-start
  65.0 289.9 %all-reduce.6.cloned.1.call-done = (bf16[256,1024]{1,0:T(8,128)(2,1)}, bf16[256,1024]{1,0:T(8,128)(2,1)}) async-done(((bf16[256,1024]{1,0:T(8,128)(2,1)}, bf16[256,1024]{1,0:T(8,128)(2,1)}), (bf16[256,1024]{1,0:T(8,128)(2,1)}, bf16[256,1024]{1,0:T(8,128)(2,1)})) %all-reduce.6.cloned.1.call-update) | async-done | bytes 1048592 | tf_op jit(solution)/shard_map/psum | solution.py:15
  354.9 3.3 convolution_bitcast_fusion
  358.2 0.0 all-reduce.4.cloned.1.call-update
  358.2 0.0 reduce-scatter.2.cloned.1.call-start
  358.3 0.1 convert_reduce_fusion
  358.4 78.5 %psum.31 = f32[32]{0:T(128)S(1)} all-reduce(f32[32]{0:T(128)S(1)} %convert_reduce_fusion), channel_id=1, replica_groups=mesh['dp'=32,'shard'=16] {'dp'}, use_global_device_ids=true, to_apply=%region_4.5 | all-reduce | flops 32 | bytes 256 | tf_op jit(solution)/shard_map/psum | solution.py:34
  436.9 0.1 select_reduce_fusion
  437.0 180.8 %all-reduce.4.cloned.1.call-done = f32[512,1024]{0,1:T(8,128)} async-done(((f32[512,1024]{0,1:T(8,128)}), f32[512,1024]{0,1:T(8,128)}) %all-reduce.4.cloned.1.call-update) | async-done | bytes 2097168 | tf_op jit(solution)/shard_map/psum | solution.py:43
  617.8 4.6 fusion.1
  622.4 0.0 reduce-scatter.2.cloned.1.call-update
  622.4 0.0 all-gather.2.cloned.1.call-start
  622.5 149.9 %reduce-scatter.2.cloned.1.call-done = f32[32,896]{1,0:T(8,128)} async-done(((f32[1024,896]{1,0:T(8,128)}), f32[32,896]{1,0:T(8,128)}) %reduce-scatter.2.cloned.1.call-update) | async-done | bytes 114704 | tf_op jit(solution)/shard_map/reduce_scatter | solution.py:46
  772.4 1.6 divide_convert_fusion
  774.0 0.0 all-gather.2.cloned.1.call-update
  774.0 67.6 %all-gather.2.cloned.1.call-done = bf16[1024,896]{1,0:T(8,128)(2,1)} async-done(((bf16[32,896]{1,0:T(8,128)(2,1)}), bf16[1024,896]{1,0:T(8,128)(2,1)}) %all-gather.2.cloned.1.call-update) | async-done | bytes 1835024 | tf_op jit(solution)/shard_map/all_gather | solution.py:55
  841.7 2.2 fusion
  843.9 1.0 copy.10
  (9 shorter events, 0.0 us)
Async XLA Ops:
  7.2 610.6 %copy-start = (bf16[512,896]{1,0:T(8,128)(2,1)S(1)}, bf16[512,896]{1,0:T(8,128)(2,1)}, u32[]{:S(2)}) copy-start(bf16[512,896]{1,0:T(8,128)(2,1)} %param.7) | copy-start | bytes 2752516
  7.2 347.7 %copy-start.1 = (bf16[512,512]{1,0:T(8,128)(2,1)S(1)}, bf16[512,512]{1,0:T(8,128)(2,1)}, u32[]{:S(2)}) copy-start(bf16[512,512]{1,0:T(8,128)(2,1)} %param.6) | copy-start | bytes 1572868
  7.2 347.7 %all-reduce.6.cloned.1.call-start = ((), (), s32[]{:S(2)}) async-start(), calls=%async_computation.4 | async-start | bytes 2097152 | tf_op jit(solution)/shard_map/psum | solution.py:15
  65.0 552.8 %all-reduce.4.cloned.1.call-start = ((), (), s32[]{:S(2)}) async-start(), calls=%async_computation.1 | async-start | bytes 4194304 | tf_op jit(solution)/shard_map/psum | solution.py:43
  354.9 3.4 copy-start.4
  358.2 414.2 %reduce-scatter.2.cloned.1.call-start = ((), (), s32[]{:S(2)}) async-start(), calls=%async_computation.2 | async-start | bytes 3784704 | tf_op jit(solution)/shard_map/reduce_scatter | solution.py:46
  622.4 150.0 %copy-start.2 = (f32[32,896]{1,0:T(8,128)S(1)}, f32[32,896]{1,0:T(8,128)}, u32[]{:S(2)}) copy-start(f32[32,896]{1,0:T(8,128)} %param.10) | copy-start | bytes 344068
  622.4 150.0 %copy-start.3 = (f32[32,896]{1,0:T(8,128)S(1)}, f32[32,896]{1,0:T(8,128)}, u32[]{:S(2)}) copy-start(f32[32,896]{1,0:T(8,128)} %param.9) | copy-start | bytes 344068
  622.4 219.2 %all-gather.2.cloned.1.call-start = ((), (), s32[]{:S(2)}) async-start(), calls=%async_computation.3 | async-start | bytes 1892352 | tf_op jit(solution)/shard_map/all_gather | solution.py:55
Sparse Core Ops, SparseCore 0:
  65.1 289.7 all-reduce.5
  358.3 259.3 all-reduce.3
  622.6 149.7 reduce-scatter.1
  775.0 66.6 all-gather.1
where the time goes:
time: 852 us; the launch traced here: 851 us
  waiting for transfers between devices  688 us (81%)
  blocking collectives  135 us (16%)
  between operations  13.8 us (2%)
  matrix products  10.1 us (1%)
    psum x1, waiting for transfers between devices, broadcast(): return lax.psum(block, axis)  290 us
    psum x1, waiting for transfers between devices, local(): projected = lax.psum(partial_value, 'shard')  181 us
    reduce_scatter x1, waiting for transfers between devices, local(): lax.psum_scatter(lax.dot_general(weighted, out_grad, contract, preferred_...  150 us
    psum x1, blocking collectives, local(): lengths = lax.psum(jnp.sum(doc_match, axis=0), 'dp')  78.5 us
    all_gather x1, waiting for transfers between devices, local(): lax.all_gather(direction, 'dp', axis=0, tiled=True)  67.6 us
    all_gather x1, blocking collectives, local(): block_rows = lax.all_gather(projector, 'shard', axis=0, tiled=True)  56.7 us
  transfers between devices with their start and end apart: 4, of which 4 were waited for; matrix products, arithmetic and copies ran while one was open for 0% of the time, Pallas kernels for 0%

commit v1 on v0

v1 whole, which is shorter than its diff:
```python
import jax
import jax.numpy as jnp
from jax import lax
from jax.experimental import pallas as pl
from jax.experimental.pallas import tpu as pltpu
from jax.sharding import PartitionSpec as P

MESH = pl.DeviceIdType.MESH
BF = jnp.bfloat16
F32 = jnp.float32

beta_first = 0.9
beta_second = 0.95
bias_first = 1.0 - beta_first**2
bias_second = 1.0 - beta_second**2
epsilon = 1e-08

TOK, FEAT, RANK, FF, ROWS = 512, 512, 1024, 896, 16
T = 4
CHUNK = TOK // T
SUB = CHUNK // 4
QUARTER = RANK // 4
MOM = 32
WIDTHS = (384, 512)
STARTS = tuple(sum(WIDTHS[:j]) for j in range(len(WIDTHS)))
N_SEM = 160


def kernel(x_hbm, g_hbm, p_hbm, m_hbm, v_hbm, ids_ref, m_out, v_out, u_out, *scratch):
    (
        x_in, g_in, m_in, v_in, rows_in, rows_up,
        part32, part, x_got, xsum32, xsum, z_got, wide, wide_t,
        count, count_got,
        loc_sem, out_sem, send_sem, recv_sem,
    ) = scratch[:20]
    per_chunk = [scratch[20 + 11 * j : 20 + 11 * (j + 1)] for j in range(len(WIDTHS))]

    d, s = lax.axis_index("dp"), lax.axis_index("shard")
    core = lax.rem(d, 2)
    zl = lax.rem(lax.div(d, 2), 4)
    y = lax.div(d, 8)
    x = lax.rem(s, 4)
    zh = lax.div(s, 4)

    def device(y=y, zl=zl, core=core, zh=zh, x=x):
        return ((y * 4 + zl) * 2 + core, zh * 4 + x)

    def up(value, k):
        return lax.rem(value + k, 4)

    other = 1 - core
    x_peers = [up(x, k) for k in (1, 3, 2)]
    y_peers = [up(y, k) for k in (1, 3, 2)]
    zl_peers = [up(zl, k) for k in (1, 3, 2)]
    zh_peers = [up(zh, k) for k in (1, 3, 2)]

    used = [0]
    sent = []

    def send(src, dst, to):
        i = used[0]
        used[0] += 1
        cp = pltpu.make_async_remote_copy(
            src_ref=src, dst_ref=dst, send_sem=send_sem.at[i], recv_sem=recv_sem.at[i],
            device_id=to, device_id_type=MESH,
        )
        cp.start()
        sent.append(cp)
        return cp

    def arrive(cps):
        for cp in cps:
            cp.wait_recv()

    own_rows = pltpu.make_async_copy(p_hbm, rows_up.at[zh, x], loc_sem.at[0])
    loads = [
        pltpu.make_async_copy(x_hbm, x_in, loc_sem.at[1]),
        pltpu.make_async_copy(g_hbm, g_in, loc_sem.at[2]),
        pltpu.make_async_copy(m_hbm, m_in, loc_sem.at[3]),
        pltpu.make_async_copy(v_hbm, v_in, loc_sem.at[4]),
    ]
    own_rows.start()
    for cp in loads:
        cp.start()

    partner = device(y=zh, zl=x, zh=y, x=zl)
    moves = jnp.logical_or(x != zl, y != zh)
    barrier = pltpu.get_barrier_semaphore()
    greet = [device(core=other)]
    greet += [device(x=p) for p in x_peers] + [device(y=p) for p in y_peers]
    greet += [device(zl=p) for p in zl_peers] + [device(zh=p) for p in zh_peers]
    for to in greet:
        pl.semaphore_signal(barrier, inc=1, device_id=to, device_id_type=MESH)

    @pl.when(moves)
    def _():
        pl.semaphore_signal(barrier, inc=1, device_id=partner, device_id_type=MESH)

    ids = jnp.transpose(jnp.broadcast_to(ids_ref[...], (128, TOK)))
    match = ids == lax.broadcasted_iota(jnp.int32, (TOK, 128), 1)
    counted = jnp.sum(match.astype(F32), axis=0, keepdims=True)
    count[0] = jnp.broadcast_to(counted, (8, 128))

    own_rows.wait()
    pl.semaphore_wait(barrier, len(greet) + moves.astype(jnp.int32))

    hop = used[0]
    used[0] += 1

    def hop_copy():
        return pltpu.make_async_remote_copy(
            src_ref=rows_up.at[zh, x], dst_ref=rows_in.at[core, zh, x],
            send_sem=send_sem.at[hop], recv_sem=recv_sem.at[hop],
            device_id=partner, device_id_type=MESH,
        )

    @pl.when(moves)
    def _():
        hop_copy().start()

    cp_c = [send(count.at[0], count_got.at[0], device(core=other))]

    @pl.when(jnp.logical_not(moves))
    def _():
        rows_in[core, zh, x] = rows_up[zh, x]

    @pl.when(moves)
    def _():
        hop_copy().wait_recv()

    cps = [send(rows_in.at[core, y, zl], rows_in.at[core, y, zl], device(zl=p)) for p in zl_peers]
    arrive(cp_c)
    count[1] = count[0] + count_got[0]
    cp_c = [send(count.at[1], count_got.at[1 + k], device(zl=p)) for k, p in enumerate(zl_peers)]
    arrive(cps)
    cps = [send(rows_in.at[core, y], rows_in.at[core, y], device(y=p)) for p in y_peers]
    arrive(cp_c)
    count[2] = count[1] + count_got[1] + count_got[2] + count_got[3]
    cp_c = [send(count.at[2], count_got.at[4 + k], device(y=p)) for k, p in enumerate(y_peers)]
    arrive(cps)
    cps = [send(rows_in.at[core], rows_in.at[core], device(core=other))]
    arrive(cp_c)
    lengths = count[2] + count_got[4] + count_got[5] + count_got[6]
    inverse = 1.0 / lengths[0:1]
    for cp in loads:
        cp.wait()
    arrive(cps)

    rhs = rows_in[...].reshape(FEAT, RANK)
    got_x, got_z, all_z, all_x = {}, {}, {}, {}

    def project(t):
        value = jnp.dot(x_in[pl.ds(t * CHUNK, CHUNK)], rhs, preferred_element_type=F32)
        for q in range(4):
            block = value[:, q * QUARTER : (q + 1) * QUARTER].reshape(4, SUB, QUARTER)
            part32[t, :, q] = block
            part[t, :, q] = block.astype(BF)
        got_x[t] = [
            send(part.at[t, p], x_got.at[t, k], device(x=p)) for k, p in enumerate(x_peers)
        ]

    def sum_x(t):
        arrive(got_x[t])
        total = part32[t, x]
        for k in range(3):
            total = total + x_got[t, k].astype(F32)
        xsum32[t] = total
        xsum[t] = total.astype(BF)
        got_z[t] = [
            send(xsum.at[t, p], z_got.at[t, k], device(zh=p)) for k, p in enumerate(zh_peers)
        ]

    def sum_z(t):
        arrive(got_z[t])
        total = xsum32[t, zh]
        for k in range(3):
            total = total + z_got[t, k].astype(F32)
        here = ids_of(t) == lax.broadcasted_iota(jnp.int32, (SUB, 128), 1)
        weight = jnp.sum(jnp.where(here, inverse, 0.0), axis=1, keepdims=True)
        wide[t, x, zh] = (total * weight).astype(BF)
        all_z[t] = [
            send(wide.at[t, x, zh], wide.at[t, x, zh], device(zh=p)) for p in zh_peers
        ]

    def ids_of(t):
        return part_ids[t, x]

    def gather_x(t):
        arrive(all_z[t])
        all_x[t] = [send(wide.at[t, x], wide.at[t, x], device(x=p)) for p in x_peers]

    def turn(t):
        arrive(all_x[t])
        for q in range(4):
            block = wide[t, :, q].reshape(CHUNK, QUARTER)
            block = jnp.transpose(block)
            for b in range(8):
                wide_t[b % 2, q * 4 + b // 2, :, t * CHUNK : (t + 1) * CHUNK] = block[
                    b * MOM : (b + 1) * MOM
                ]

    part_ids = scratch[-1]
    part_ids[...] = ids.reshape(T, 4, SUB, 128)
    stages = (project, sum_x, sum_z, gather_x, turn)
    for t in range(T):
        project(t)
    for step in range(T + 3):
        for stage in (1, 2, 3, 4):
            t = step - (stage - 1)
            if 0 <= t < T:
                stages[stage](t)

    up_z = [send(rows_up.at[zh, x], rows_up.at[zh, x], device(zh=p)) for p in zh_peers]
    up_x = []
    outs = []
    got = {}

    def gradient(j):
        g_own, g_peer, c_got = per_chunk[j][0:3]
        cols = pl.ds(STARTS[j], WIDTHS[j])
        lhs = wide_t[other].reshape(RANK // 2, TOK)
        value = jnp.dot(lhs, g_in[:, cols], preferred_element_type=F32)
        g_peer[...] = value.astype(BF).reshape(4, 4, MOM, WIDTHS[j])
        got["c", j] = [send(g_peer, c_got, device(core=other))]
        lhs = wide_t[core].reshape(RANK // 2, TOK)
        value = jnp.dot(lhs, g_in[:, cols], preferred_element_type=F32)
        g_own[...] = value.reshape(4, 4, MOM, WIDTHS[j])

    def sum_core(j):
        g_own, _, c_got, ysum, y_got = per_chunk[j][0:5]
        arrive(got["c", j])
        for k, p in enumerate(y_peers):
            ysum[k] = (g_own[p] + c_got[p].astype(F32)).astype(BF)
            got["y", j, k] = [send(ysum.at[k], y_got.at[k], device(y=p))]

    def sum_y(j):
        g_own, _, c_got, ysum, y_got, zsum32, zsum, l_got = per_chunk[j][0:8]
        total = g_own[y] + c_got[y].astype(F32)
        for k in range(3):
            arrive(got["y", j, k])
            total = total + y_got[k].astype(F32)
        zsum32[...] = total
        zsum[...] = total.astype(BF)
        got["l", j] = [
            send(zsum.at[p], l_got.at[k], device(zl=p)) for k, p in enumerate(zl_peers)
        ]

    def adam(j):
        zsum32, _, l_got, full, m_new, v_new = per_chunk[j][5:11]
        cols = pl.ds(STARTS[j], WIDTHS[j])
        arrive(got["l", j])
        grad = zsum32[zl]
        for k in range(3):
            grad = grad + l_got[k].astype(F32)
        first = beta_first * m_in[:, cols] + (1.0 - beta_first) * grad
        second = beta_second * v_in[:, cols] + (1.0 - beta_second) * (grad * grad)
        way = first / bias_first / (jnp.sqrt(second / bias_second) + epsilon)
        full[y, zl, core] = way.astype(BF)
        got["dl", j] = [
            send(full.at[y, zl, core], full.at[y, zl, core], device(zl=p)) for p in zl_peers
        ]
        m_new[...] = first
        v_new[...] = second
        for value, out in ((m_new, m_out), (v_new, v_out)):
            cp = pltpu.make_async_copy(value, out.at[:, cols], out_sem.at[len(outs)])
            cp.start()
            outs.append(cp)

    def gather_y(j):
        full = per_chunk[j][8]
        arrive(got["dl", j])
        got["dy", j] = [
            send(full.at[y, :, core], full.at[y, :, core], device(y=p)) for p in y_peers
        ]

    def gather_core(j):
        full = per_chunk[j][8]
        arrive(got["dy", j])
        got["dc", j] = [send(full.at[:, :, core], full.at[:, :, core], device(core=other))]

    def update(j):
        full, u_new = per_chunk[j][8], u_parts[j]
        cols = pl.ds(STARTS[j], WIDTHS[j])
        arrive(got["dc", j])
        lhs = rows_up[...].reshape(256, RANK)
        value = jnp.dot(lhs, full[...].reshape(RANK, WIDTHS[j]), preferred_element_type=F32)
        u_new[...] = value.astype(BF)
        cp = pltpu.make_async_copy(u_new, u_out.at[:, cols], out_sem.at[len(outs)])
        cp.start()
        outs.append(cp)

    u_parts = scratch[20 + 11 * len(WIDTHS) : 20 + 12 * len(WIDTHS)]
    stages = (gradient, sum_core, sum_y, adam, gather_y, gather_core, update)
    n = len(WIDTHS)
    for step in range(n + len(stages) - 1):
        for stage in range(len(stages)):
            j = step - stage
            if 0 <= j < n:
                if stage == 3 and j == 0:
                    arrive(up_z)
                    up_x += [
                        send(rows_up.at[:, x], rows_up.at[:, x], device(x=p)) for p in x_peers
                    ]
                if stage == 6 and j == 0:
                    arrive(up_x)
                stages[stage](j)

    @pl.when(moves)
    def _():
        hop_copy().wait_send()

    for cp in sent:
        cp.wait_send()
    for cp in outs:
        cp.wait()


def local(layer_input, out_grad, projector, first_moment, second_moment, doc_ids):
    scratch = [
        pltpu.VMEM((TOK, FEAT), BF),
        pltpu.VMEM((TOK, FF), BF),
        pltpu.VMEM((MOM, FF), F32),
        pltpu.VMEM((MOM, FF), F32),
        pltpu.VMEM((2, 4, 4, ROWS, RANK), BF),
        pltpu.VMEM((4, 4, ROWS, RANK), BF),
        pltpu.VMEM((T, 4, 4, SUB, QUARTER), F32),
        pltpu.VMEM((T, 4, 4, SUB, QUARTER), BF),
        pltpu.VMEM((T, 3, 4, SUB, QUARTER), BF),
        pltpu.VMEM((T, 4, SUB, QUARTER), F32),
        pltpu.VMEM((T, 4, SUB, QUARTER), BF),
        pltpu.VMEM((T, 3, SUB, QUARTER), BF),
        pltpu.VMEM((T, 4, 4, SUB, QUARTER), BF),
        pltpu.VMEM((2, 16, MOM, TOK), BF),
        pltpu.VMEM((3, 8, 128), F32),
        pltpu.VMEM((7, 8, 128), F32),
        pltpu.SemaphoreType.DMA((5,)),
        pltpu.SemaphoreType.DMA((3 * len(WIDTHS),)),
        pltpu.SemaphoreType.DMA((N_SEM,)),
        pltpu.SemaphoreType.DMA((N_SEM,)),
    ]
    for w in WIDTHS:
        scratch += [
            pltpu.VMEM((4, 4, MOM, w), F32),
            pltpu.VMEM((4, 4, MOM, w), BF),
            pltpu.VMEM((4, 4, MOM, w), BF),
            pltpu.VMEM((3, 4, MOM, w), BF),
            pltpu.VMEM((3, 4, MOM, w), BF),
            pltpu.VMEM((4, MOM, w), F32),
            pltpu.VMEM((4, MOM, w), BF),
            pltpu.VMEM((3, MOM, w), BF),
            pltpu.VMEM((4, 4, 2, MOM, w), BF),
            pltpu.VMEM((MOM, w), F32),
            pltpu.VMEM((MOM, w), F32),
        ]
    scratch += [pltpu.VMEM((256, w), BF) for w in WIDTHS]
    scratch += [pltpu.VMEM((T, 4, SUB, 128), jnp.int32)]
    any_space = pl.BlockSpec(memory_space=pl.ANY)
    return pl.pallas_call(
        kernel,
        out_shape=(
            jax.ShapeDtypeStruct((MOM, FF), F32),
            jax.ShapeDtypeStruct((MOM, FF), F32),
            jax.ShapeDtypeStruct((256, FF), BF),
        ),
        in_specs=[any_space] * 5 + [pl.BlockSpec(memory_space=pltpu.VMEM)],
        out_specs=(any_space,) * 3,
        scratch_shapes=scratch,
        compiler_params=pltpu.CompilerParams(
            collective_id=0, has_side_effects=True, vmem_limit_bytes=56 * 2**20
        ),
        cost_estimate=pl.CostEstimate(flops=2 * 10**9, bytes_accessed=4 * 10**6, transcendentals=0),
        name="galore",
    )(layer_input, out_grad, projector, first_moment, second_moment, doc_ids.reshape(1, TOK))


def solution(mesh):
    placed = (
        P("dp", "shard"),
        P("dp", "shard"),
        P(("dp", "shard"), None),
        P("dp", "shard"),
        P("dp", "shard"),
        P("dp"),
    )
    return jax.shard_map(
        local,
        mesh=mesh,
        in_specs=placed,
        out_specs=(P("dp", "shard"), P("dp", "shard"), P("dp", "shard")),
        check_vma=False,
    )
```

time: 852 us -> 126 us (0.15)
  waiting for transfers between devices: 688 us -> 0 us
  blocking collectives: 135 us -> 0 us
  Pallas kernels: 0 us -> 122 us
  between operations: 13.8 us -> 0.65 us
  matrix products: 10.1 us -> 0 us
    psum x2 -> x0, waiting for transfers between devices: 471 us -> none  [the longest x1 290 us: broadcast(): return lax.psum(block, axis)]
    reduce_scatter x1 -> x0, waiting for transfers between devices: 150 us -> none  [local(): lax.psum_scatter(lax.dot_general(weighted, out_grad, contract, preferred_...]
    pallas_call x0 -> x1, Pallas kernels: none -> 122 us  [local(): pl.pallas_call(kernel, out_shape=(jax.ShapeDtypeStruct((MOM, FF), F32), j...]
    psum x1 -> x0, blocking collectives: 78.5 us -> none  [local(): lengths = lax.psum(jnp.sum(doc_match, axis=0), 'dp')]
    all_gather x1 -> x0, waiting for transfers between devices: 67.6 us -> none  [local(): lax.all_gather(direction, 'dp', axis=0, tiled=True)]
    all_gather x1 -> x0, blocking collectives: 56.7 us -> none  [local(): block_rows = lax.all_gather(projector, 'shard', axis=0, tiled=True)]
    dot_general x3 -> x0, matrix products: 10.1 us -> none  [the longest x1 4.62 us: local(): lax.dot_general(weighted, out_grad, contract, preferred_element_type=jnp....]
  transfers between devices with their start and end apart: 4 -> 0, of which waited for: 4 -> 0; matrix products, arithmetic and copies ran while one was open for 0% -> 0% of each run, Pallas kernels for 0% -> 0%
where the time goes in v1:
time: 126 us
  Pallas kernels  122 us (97%)
  local copies, waits for them, and re-layouts  3.93 us (3%)
    pallas_call x1, Pallas kernels, local(): pl.pallas_call(kernel, out_shape=(jax.ShapeDtypeStruct((MOM, FF), F32), j...  122 us
    unnamed x5, local copies, waits for them, and re-layouts  3.93 us

profile of v1, /device:TPU:1, one launch (start us, length us, event | category | flops | bytes accessed | tf_op | source)
XLA Modules:
  0.0 126.3 jit_solution(13346197295249843987)
XLA Ops:
  0.6 121.7 %galore.1 = (f32[32,896]{1,0:T(8,128)}, f32[32,896]{1,0:T(8,128)}, bf16[256,896]{1,0:T(8,128)(2,1)}) custom-call(bf16[512,512]{1,0:T(8,128)(2,1)} %x_hbm.1, bf16[512,896]{1,0:T(8,128)(2,1)} %g_hbm.1, bf16[16,1024]{1,0:T(8,128)(2,1)} %p_hbm.1, f32[32,896]{1,0:T(8,128)} %m_hbm.1, f32[32,896]{1,0:T(8,128)} %v_hbm.1, s32[1,512]{1,0:T(1,128)} %bitcast.1), custom_call_target="tpu_custom_call" | custom-call | flops 2000000000 | bytes 4000000 | tf_op jit(solution)/shard_map/galore/pallas_call | solution.py:358
  122.3 0.0 copy-start
  122.3 1.6 %copy.12 = f32[32,896]{1,0:T(8,128)} copy(f32[32,896]{1,0:T(8,128)} %get-tuple-element.6) | data formatting | bytes 229376
  124.0 1.6 %copy.13 = f32[32,896]{1,0:T(8,128)} copy(f32[32,896]{1,0:T(8,128)} %get-tuple-element.7) | data formatting | bytes 229376
  125.5 0.0 copy-done
  125.5 0.8 copy.14
Async XLA Ops:
  122.3 3.2 %copy-start = (bf16[256,896]{1,0:T(8,128)(2,1)S(1)}, bf16[256,896]{1,0:T(8,128)(2,1)}, u32[]{:S(2)}) copy-start(bf16[256,896]{1,0:T(8,128)(2,1)} %get-tuple-element.8) | copy-start | bytes 1376260

commit v2 on v0

v2 whole, which is shorter than its diff:
```python
import jax
import jax.numpy as jnp
from jax import lax
from jax.experimental import pallas as pl
from jax.experimental.pallas import tpu as pltpu
from jax.sharding import PartitionSpec as P

MESH = pl.DeviceIdType.MESH
BF = jnp.bfloat16
F32 = jnp.float32

beta_first = 0.9
beta_second = 0.95
bias_first = 1.0 - beta_first**2
bias_second = 1.0 - beta_second**2
epsilon = 1e-08

TOK, FEAT, RANK, FF, ROWS, MOM = 512, 512, 1024, 896, 16, 32
HALF = RANK // 2
QUARTER = RANK // 4
SUB = TOK // 16
PARTS = ((0, 0, 896), (1, 0, 384), (1, 384, 512))
N_PARTS = len(PARTS)
ORDER = (
    ("cnt", 0), ("hop", 0), ("cnt", 1), ("hop", 1), ("cnt", 2), ("zl", 0), ("zl", 1), ("y", 0), ("mm", 0),
    ("mm", 1), ("y", 1), ("mm", 3), ("mm", 2), ("sx", 0), ("sx", 1), ("sx", 3), ("sz", 0), ("sx", 2),
    ("sz", 1), ("sz", 3), ("gx", 0), ("sz", 2), ("gx", 1), ("turn", 0), ("gx", 3), ("fz",), ("gx", 2),
    ("turn", 1), ("mm2", 0), ("turn", 3), ("sc", 0), ("turn", 2), ("mm2", 2), ("mm2", 1), ("fx",), ("sc", 2),
    ("sc", 1), ("sy", 0), ("sy", 2), ("sy", 1), ("adam", 0), ("adam", 2), ("adam", 1), ("gy", 0), ("gy", 2),
    ("gy", 1), ("gc", 0), ("up", 0), ("gc", 2), ("gc", 1), ("up", 2), ("up", 1),
)
N_SEM = 31 + 6 * N_PARTS
N_FIXED = 21
N_EACH = 9


def kernel(x_hbm, g_hbm, p_hbm, m_hbm, v_hbm, ids_ref, m_out, v_out, u_out, *scratch):
    (
        x_in, g_in, m_in, v_in, p_in, rows_in, rows_up,
        part32, part, x_got, xsum32, xsum, z_got, wide, wide_t,
        count, count_got, u_sum,
        loc_sem, send_sem, recv_sem,
    ) = scratch[:N_FIXED]
    of_part = [scratch[N_FIXED + N_EACH * e : N_FIXED + N_EACH * (e + 1)] for e in range(N_PARTS)]
    m_new, v_new, u_new, weights = scratch[N_FIXED + N_EACH * N_PARTS :]

    d, s = lax.axis_index("dp"), lax.axis_index("shard")
    core = lax.rem(d, 2)
    zl = lax.rem(lax.div(d, 2), 4)
    y = lax.div(d, 8)
    x = lax.rem(s, 4)
    zh = lax.div(s, 4)

    def device(y=y, zl=zl, core=core, zh=zh, x=x):
        return ((y * 4 + zl) * 2 + core, zh * 4 + x)

    def up(value, k):
        return lax.rem(value + k, 4)

    other = 1 - core
    x_peers = [up(x, k) for k in (1, 3, 2)]
    y_peers = [up(y, k) for k in (1, 3, 2)]
    zl_peers = [up(zl, k) for k in (1, 3, 2)]
    zh_peers = [up(zh, k) for k in (1, 3, 2)]

    used = [0]
    flying = {}
    groups = []

    def send(name, whole, copies):
        i = used[0]
        used[0] += 1
        for src, dst, to in copies:
            pltpu.make_async_remote_copy(
                src_ref=src, dst_ref=dst, send_sem=send_sem.at[i], recv_sem=recv_sem.at[i],
                device_id=to, device_id_type=MESH,
            ).start()
        flying[name] = (whole, i)
        groups.append((whole, i))

    def arrive(name):
        whole, i = flying.pop(name)
        pltpu.make_async_copy(whole, whole, recv_sem.at[i]).wait()

    own_rows = pltpu.make_async_copy(p_hbm, p_in, loc_sem.at[0])
    loads = [
        pltpu.make_async_copy(x_hbm, x_in, loc_sem.at[1]),
        pltpu.make_async_copy(g_hbm, g_in, loc_sem.at[2]),
        pltpu.make_async_copy(m_hbm, m_in, loc_sem.at[3]),
        pltpu.make_async_copy(v_hbm, v_in, loc_sem.at[4]),
    ]
    own_rows.start()
    for cp in loads:
        cp.start()

    to_hop = device(y=up(zh, y), zl=x, zh=y, x=zl)
    seat = up(y, 4 - zh)
    from_hop = device(y=zh, zl=x, zh=seat, x=zl)
    moves = jnp.logical_or(x != zl, jnp.logical_or(y != 0, zh != 0))
    barrier = pltpu.get_barrier_semaphore()
    greet = [device(core=other)]
    greet += [device(x=p) for p in x_peers] + [device(y=p) for p in y_peers]
    greet += [device(zl=p) for p in zl_peers] + [device(zh=p) for p in zh_peers]
    for to in greet:
        pl.semaphore_signal(barrier, inc=1, device_id=to, device_id_type=MESH)

    @pl.when(moves)
    def _():
        pl.semaphore_signal(barrier, inc=1, device_id=from_hop, device_id_type=MESH)

    own_rows.wait()
    held = p_in[...].astype(F32)
    turned = [held] + [jnp.concatenate([held[:, k:], held[:, :k]], axis=1) for k in (32, 16, 48)]
    turned = jnp.concatenate(turned, axis=0).astype(BF)
    at = lax.broadcasted_iota(jnp.int32, (RANK, QUARTER), 0)
    col = lax.broadcasted_iota(jnp.int32, (1, QUARTER), 1)
    pick = (at == (col >> 4) * 64 + (col & 15)).astype(F32).astype(BF)
    moved = jnp.dot(turned, pick, preferred_element_type=F32).astype(BF)
    for r in range(4):
        h, c = divmod(r, 2)
        rows_up[h, zh, x, :, c * QUARTER : (c + 1) * QUARTER] = moved[r * ROWS : (r + 1) * ROWS]

    ids = jnp.transpose(jnp.broadcast_to(ids_ref[...], (128, TOK)))
    match = (ids == lax.broadcasted_iota(jnp.int32, (TOK, 128), 1)).astype(F32)
    count[0] = jnp.broadcast_to(jnp.sum(match, axis=0, keepdims=True), (8, 128))

    pl.semaphore_wait(barrier, len(greet) + moves.astype(jnp.int32))

    def hop(h):
        return pltpu.make_async_remote_copy(
            src_ref=rows_up.at[h, zh, x], dst_ref=rows_in.at[h, core, zh, x],
            send_sem=send_sem.at[N_SEM - 1 - h], recv_sem=recv_sem.at[N_SEM - 1 - h],
            device_id=to_hop, device_id_type=MESH,
        )

    @pl.when(moves)
    def _():
        hop(0).start()
        hop(1).start()

    send(("CNT", 0), count_got.at[0], [(count.at[0], count_got.at[0], device(core=other))])

    @pl.when(jnp.logical_not(moves))
    def _():
        for h in range(2):
            rows_in[h, core, zh, x] = rows_up[h, zh, x]

    def do_cnt(i):
        if i == 0:
            arrive(("CNT", 0))
            count[1] = count[0] + count_got[0]
            send(("cnt", 0), count_got.at[pl.ds(1, 3)], [
                (count.at[1], count_got.at[1 + k], device(zl=p)) for k, p in enumerate(zl_peers)
            ])
        elif i == 1:
            arrive(("cnt", 0))
            count[2] = count[1] + count_got[1] + count_got[2] + count_got[3]
            send(("cnt", 1), count_got.at[pl.ds(4, 3)], [
                (count.at[2], count_got.at[4 + k], device(y=p)) for k, p in enumerate(y_peers)
            ])
        else:
            arrive(("cnt", 1))
            lengths = count[2] + count_got[4] + count_got[5] + count_got[6]
            inverse = 1.0 / lengths[0:1]
            mine = ids_ref[:, pl.ds(pl.multiple_of(x * 128, 128), 128)]
            mine = jnp.transpose(jnp.broadcast_to(mine, (128, 128)))
            here = mine == lax.broadcasted_iota(jnp.int32, (128, 128), 1)
            weight = jnp.sum(jnp.where(here, inverse, 0.0), axis=1, keepdims=True)
            weights[...] = jnp.broadcast_to(weight, (128, 128)).reshape(4, SUB, 128)

    def do_hop(h):
        @pl.when(moves)
        def _():
            hop(h).wait_recv()

        mine = rows_in.at[h, core, seat, zl]
        send(("hop", h), rows_in.at[h, core, 0, pl.ds(0, 3)], [
            (mine, mine, device(zl=p)) for p in zl_peers
        ])

    def do_zl(h):
        arrive(("hop", h))
        mine = rows_in.at[h, core, seat]
        send(("zl", h), rows_in.at[h, core, pl.ds(0, 3)], [
            (mine, mine, device(y=p)) for p in y_peers
        ])

    def do_y(h):
        arrive(("zl", h))
        mine = rows_in.at[h, core]
        send(("y", h), mine, [(mine, mine, device(core=other))])

    def do_mm(r):
        h, c = divmod(r, 2)
        if ("y", h) in flying:
            arrive(("y", h))
        if loads:
            for cp in loads:
                cp.wait()
            loads.clear()
        rhs = rows_in[h].reshape(FEAT, HALF)[:, c * QUARTER : (c + 1) * QUARTER]
        value = jnp.dot(x_in[...], rhs, preferred_element_type=F32).reshape(4, 4, SUB, QUARTER)
        part32[r] = value
        part[r] = value.astype(BF)
        send(("mm", r), x_got.at[r], [
            (part.at[r, p], x_got.at[r, k], device(x=p)) for k, p in enumerate(x_peers)
        ])

    def do_sx(r):
        arrive(("mm", r))
        total = part32[r, x]
        for k in range(3):
            total = total + x_got[r, k].astype(F32)
        xsum32[r] = total
        xsum[r] = total.astype(BF)
        send(("sx", r), z_got.at[r], [
            (xsum.at[r, p], z_got.at[r, k], device(zh=p)) for k, p in enumerate(zh_peers)
        ])

    def do_sz(r):
        arrive(("sx", r))
        total = xsum32[r, zh]
        for k in range(3):
            total = total + z_got[r, k].astype(F32)
        wide[r, x, zh] = (total * weights[zh][:, 0:1]).astype(BF)
        mine = wide.at[r, x, zh]
        send(("sz", r), wide.at[r, x, pl.ds(0, 3)], [(mine, mine, device(zh=p)) for p in zh_peers])

    def do_gx(r):
        arrive(("sz", r))
        mine = wide.at[r, x]
        send(("gx", r), wide.at[r, pl.ds(0, 3)], [(mine, mine, device(x=p)) for p in x_peers])

    def do_turn(r):
        arrive(("gx", r))
        wide_t[r] = jnp.transpose(wide[r].reshape(TOK, QUARTER))

    def do_fz():
        mine = rows_up.at[:, zh, x]
        send(("fz",), rows_up.at[:, pl.ds(0, 3), x], [(mine, mine, device(zh=p)) for p in zh_peers])

    def do_fx():
        arrive(("fz",))
        mine = rows_up.at[:, :, x]
        send(("fx",), rows_up.at[:, :, pl.ds(0, 3)], [(mine, mine, device(x=p)) for p in x_peers])

    def do_mm2(e):
        h, start, width = PARTS[e]
        g_own, g_peer, c_got = of_part[e][0:3]
        cols = pl.ds(start, width)
        value = jnp.dot(wide_t[2 * h + other], g_in[:, cols], preferred_element_type=F32)
        g_peer[...] = value.astype(BF).reshape(4, 4, 16, width)
        send(("mm2", e), c_got, [(g_peer, c_got, device(core=other))])
        value = jnp.dot(wide_t[2 * h + core], g_in[:, cols], preferred_element_type=F32)
        g_own[...] = value.reshape(4, 4, 16, width)

    def do_sc(e):
        g_own, _, c_got, ysum, y_got = of_part[e][0:5]
        arrive(("mm2", e))
        for k, p in enumerate(y_peers):
            ysum[k] = (g_own[p] + c_got[p].astype(F32)).astype(BF)
        send(("sc", e), y_got, [
            (ysum.at[k], y_got.at[k], device(y=p)) for k, p in enumerate(y_peers)
        ])

    def do_sy(e):
        g_own, _, c_got, _, y_got, zsum32, zsum, l_got = of_part[e][0:8]
        total = g_own[y] + c_got[y].astype(F32)
        arrive(("sc", e))
        for k in range(3):
            total = total + y_got[k].astype(F32)
        zsum32[...] = total
        zsum[...] = total.astype(BF)
        send(("sy", e), l_got, [
            (zsum.at[p], l_got.at[k], device(zl=p)) for k, p in enumerate(zl_peers)
        ])

    def do_adam(e):
        h, start, width = PARTS[e]
        zsum32, _, l_got, full = of_part[e][5:9]
        rows, cols = pl.ds(h * 16, 16), pl.ds(start, width)
        arrive(("sy", e))
        grad = zsum32[zl]
        for k in range(3):
            grad = grad + l_got[k].astype(F32)
        first = beta_first * m_in[rows, cols] + (1.0 - beta_first) * grad
        second = beta_second * v_in[rows, cols] + (1.0 - beta_second) * (grad * grad)
        way = first / bias_first / (jnp.sqrt(second / bias_second) + epsilon)
        full[core, y, zl] = way.astype(BF)
        mine = full.at[core, y, zl]
        send(("adam", e), full.at[core, y, pl.ds(0, 3)], [
            (mine, mine, device(zl=p)) for p in zl_peers
        ])
        m_new[rows, cols] = first
        v_new[rows, cols] = second

    def do_gy(e):
        full = of_part[e][8]
        arrive(("adam", e))
        mine = full.at[core, y]
        send(("gy", e), full.at[core, pl.ds(0, 3)], [(mine, mine, device(y=p)) for p in y_peers])

    def do_gc(e):
        full = of_part[e][8]
        arrive(("gy", e))
        mine = full.at[core]
        send(("gc", e), mine, [(mine, mine, device(core=other))])

    def do_up(e):
        h, start, width = PARTS[e]
        full = of_part[e][8]
        if ("fx",) in flying:
            arrive(("fx",))
        arrive(("gc", e))
        lhs = rows_up[h].reshape(256, HALF)
        value = jnp.dot(lhs, full[...].reshape(HALF, width), preferred_element_type=F32)
        if h == 0:
            u_sum[:, pl.ds(start, width)] = value
        else:
            value = value + u_sum[:, pl.ds(start, width)]
            u_new[:, pl.ds(start, width)] = value.astype(BF)

    steps = {
        "hop": do_hop, "zl": do_zl, "y": do_y, "cnt": do_cnt, "mm": do_mm, "sx": do_sx,
        "sz": do_sz, "gx": do_gx, "turn": do_turn, "fz": do_fz, "fx": do_fx, "mm2": do_mm2,
        "sc": do_sc, "sy": do_sy, "adam": do_adam, "gy": do_gy, "gc": do_gc, "up": do_up,
    }
    for name, *which in ORDER:
        steps[name](*which)

    outs = [
        pltpu.make_async_copy(value, out, loc_sem.at[i])
        for i, (value, out) in enumerate(((m_new, m_out), (v_new, v_out), (u_new, u_out)))
    ]
    for cp in outs:
        cp.start()

    @pl.when(moves)
    def _():
        hop(0).wait_send()
        hop(1).wait_send()

    for whole, i in groups:
        pltpu.make_async_copy(whole, whole, send_sem.at[i]).wait()
    for cp in outs:
        cp.wait()


def hand_on(m_in, v_in, u_in, m_out, v_out, u_out, m_held, v_held, u_held, sem):
    ways = ((m_in, m_held, m_out), (v_in, v_held, v_out), (u_in, u_held, u_out))
    reads = [pltpu.make_async_copy(a, b, sem.at[i]) for i, (a, b, _) in enumerate(ways)]
    writes = [pltpu.make_async_copy(b, c, sem.at[3 + i]) for i, (_, b, c) in enumerate(ways)]
    for cp in reads:
        cp.start()
    for read, write in zip(reads, writes):
        read.wait()
        write.start()
    for cp in writes:
        cp.wait()


def local(layer_input, out_grad, projector, first_moment, second_moment, doc_ids):
    scratch = [
        pltpu.VMEM((TOK, FEAT), BF),
        pltpu.VMEM((TOK, FF), BF),
        pltpu.VMEM((MOM, FF), F32),
        pltpu.VMEM((MOM, FF), F32),
        pltpu.VMEM((ROWS, RANK), BF),
        pltpu.VMEM((2, 2, 4, 4, ROWS, HALF), BF),
        pltpu.VMEM((2, 4, 4, ROWS, HALF), BF),
        pltpu.VMEM((4, 4, 4, SUB, QUARTER), F32),
        pltpu.VMEM((4, 4, 4, SUB, QUARTER), BF),
        pltpu.VMEM((4, 3, 4, SUB, QUARTER), BF),
        pltpu.VMEM((4, 4, SUB, QUARTER), F32),
        pltpu.VMEM((4, 4, SUB, QUARTER), BF),
        pltpu.VMEM((4, 3, SUB, QUARTER), BF),
        pltpu.VMEM((4, 4, 4, SUB, QUARTER), BF),
        pltpu.VMEM((4, QUARTER, TOK), BF),
        pltpu.VMEM((3, 8, 128), F32),
        pltpu.VMEM((7, 8, 128), F32),
        pltpu.VMEM((256, FF), F32),
        pltpu.SemaphoreType.DMA((5,)),
        pltpu.SemaphoreType.DMA((N_SEM,)),
        pltpu.SemaphoreType.DMA((N_SEM,)),
    ]
    for _, _, w in PARTS:
        scratch += [
            pltpu.VMEM((4, 4, 16, w), F32),
            pltpu.VMEM((4, 4, 16, w), BF),
            pltpu.VMEM((4, 4, 16, w), BF),
            pltpu.VMEM((3, 4, 16, w), BF),
            pltpu.VMEM((3, 4, 16, w), BF),
            pltpu.VMEM((4, 16, w), F32),
            pltpu.VMEM((4, 16, w), BF),
            pltpu.VMEM((3, 16, w), BF),
            pltpu.VMEM((2, 4, 4, 16, w), BF),
        ]
    scratch += [
        pltpu.VMEM((MOM, FF), F32),
        pltpu.VMEM((MOM, FF), F32),
        pltpu.VMEM((256, FF), BF),
        pltpu.VMEM((4, SUB, 128), F32),
    ]
    any_space = pl.BlockSpec(memory_space=pl.ANY)
    results = (
        jax.ShapeDtypeStruct((MOM, FF), F32),
        jax.ShapeDtypeStruct((MOM, FF), F32),
        jax.ShapeDtypeStruct((256, FF), BF),
    )
    made = pl.pallas_call(
        kernel,
        out_shape=results,
        in_specs=[any_space] * 5 + [pl.BlockSpec(memory_space=pltpu.VMEM)],
        out_specs=(any_space,) * 3,
        scratch_shapes=scratch,
        compiler_params=pltpu.CompilerParams(
            collective_id=0, has_side_effects=True, vmem_limit_bytes=56 * 2**20
        ),
        cost_estimate=pl.CostEstimate(flops=2 * 10**9, bytes_accessed=4 * 10**6, transcendentals=0),
        name="galore",
    )(layer_input, out_grad, projector, first_moment, second_moment, doc_ids.reshape(1, TOK))
    return pl.pallas_call(
        hand_on,
        out_shape=results,
        in_specs=[any_space] * 3,
        out_specs=(any_space,) * 3,
        scratch_shapes=[
            pltpu.VMEM((MOM, FF), F32),
            pltpu.VMEM((MOM, FF), F32),
            pltpu.VMEM((256, FF), BF),
            pltpu.SemaphoreType.DMA((6,)),
        ],
        compiler_params=pltpu.CompilerParams(vmem_limit_bytes=56 * 2**20),
        name="hand_on",
    )(*made)


def solution(mesh):
    placed = (
        P("dp", "shard"),
        P("dp", "shard"),
        P(("dp", "shard"), None),
        P("dp", "shard"),
        P("dp", "shard"),
        P("dp"),
    )
    return jax.shard_map(
        local,
        mesh=mesh,
        in_specs=placed,
        out_specs=(P("dp", "shard"), P("dp", "shard"), P("dp", "shard")),
        check_vma=False,
    )
```

time: 852 us -> 110 us (0.13)
  waiting for transfers between devices: 688 us -> 0 us
  blocking collectives: 135 us -> 0 us
  Pallas kernels: 0 us -> 109 us
  between operations: 13.8 us -> 0.64 us
  matrix products: 10.1 us -> 0 us
    psum x2 -> x0, waiting for transfers between devices: 471 us -> none  [the longest x1 290 us: broadcast(): return lax.psum(block, axis)]
    reduce_scatter x1 -> x0, waiting for transfers between devices: 150 us -> none  [local(): lax.psum_scatter(lax.dot_general(weighted, out_grad, contract, preferred_...]
    pallas_call x0 -> x2, Pallas kernels: none -> 109 us  [the longest x1 107 us: local(): pl.pallas_call(kernel, out_shape=results, in_specs=[any_space] * 5 + [pl....]
    psum x1 -> x0, blocking collectives: 78.5 us -> none  [local(): lengths = lax.psum(jnp.sum(doc_match, axis=0), 'dp')]
    all_gather x1 -> x0, waiting for transfers between devices: 67.6 us -> none  [local(): lax.all_gather(direction, 'dp', axis=0, tiled=True)]
    all_gather x1 -> x0, blocking collectives: 56.7 us -> none  [local(): block_rows = lax.all_gather(projector, 'shard', axis=0, tiled=True)]
    dot_general x3 -> x0, matrix products: 10.1 us -> none  [the longest x1 4.62 us: local(): lax.dot_general(weighted, out_grad, contract, preferred_element_type=jnp....]
  transfers between devices with their start and end apart: 4 -> 0, of which waited for: 4 -> 0; matrix products, arithmetic and copies ran while one was open for 0% -> 0% of each run, Pallas kernels for 0% -> 0%
where the time goes in v2:
time: 110 us; the launch traced here: 109 us
  Pallas kernels  109 us (99%)
    pallas_call x1, Pallas kernels, local(): pl.pallas_call(kernel, out_shape=results, in_specs=[any_space] * 5 + [pl....  107 us

profile of v2, /device:TPU:1, one launch (start us, length us, event | category | flops | bytes accessed | tf_op | source)
XLA Modules:
  0.0 109.4 jit_solution(2130623639957485890)
XLA Ops:
  0.6 106.8 %galore.1 = (f32[32,896]{1,0:T(8,128)}, f32[32,896]{1,0:T(8,128)}, bf16[256,896]{1,0:T(8,128)(2,1)}) custom-call(bf16[512,512]{1,0:T(8,128)(2,1)} %x_hbm.1, bf16[512,896]{1,0:T(8,128)(2,1)} %g_hbm.1, bf16[16,1024]{1,0:T(8,128)(2,1)} %p_hbm.1, f32[32,896]{1,0:T(8,128)} %m_hbm.1, f32[32,896]{1,0:T(8,128)} %v_hbm.1, s32[1,512]{1,0:T(1,128)} %bitcast.1), custom_call_target="tpu_custom_call" | custom-call | flops 2000000000 | bytes 4000000 | tf_op jit(solution)/shard_map/galore/pallas_call | solution.py:410
  107.5 2.0 %hand_on.1 = (f32[32,896]{1,0:T(8,128)}, f32[32,896]{1,0:T(8,128)}, bf16[256,896]{1,0:T(8,128)(2,1)}) custom-call(f32[32,896]{1,0:T(8,128)} %get-tuple-element.6.m_in, f32[32,896]{1,0:T(8,128)} %get-tuple-element.7.v_in, bf16[256,896]{1,0:T(8,128)(2,1)} %get-tuple-element.8.u_in), custom_call_target="tpu_custom_call" | custom-call | tf_op jit(solution)/shard_map/hand_on/pallas_call | solution.py:422

commit v3 on v2

--- a/solution.py
+++ b/solution.py
@@ -22,23 +22,23 @@
 PARTS = ((0, 0, 896), (1, 0, 384), (1, 384, 512))
 N_PARTS = len(PARTS)
 ORDER = (
-    ("cnt", 0), ("hop", 0), ("cnt", 1), ("hop", 1), ("cnt", 2), ("zl", 0), ("zl", 1), ("y", 0), ("mm", 0),
-    ("mm", 1), ("y", 1), ("mm", 3), ("mm", 2), ("sx", 0), ("sx", 1), ("sx", 3), ("sz", 0), ("sx", 2),
-    ("sz", 1), ("sz", 3), ("gx", 0), ("sz", 2), ("gx", 1), ("turn", 0), ("gx", 3), ("fz",), ("gx", 2),
-    ("turn", 1), ("mm2", 0), ("turn", 3), ("sc", 0), ("turn", 2), ("mm2", 2), ("mm2", 1), ("fx",), ("sc", 2),
-    ("sc", 1), ("sy", 0), ("sy", 2), ("sy", 1), ("adam", 0), ("adam", 2), ("adam", 1), ("gy", 0), ("gy", 2),
-    ("gy", 1), ("gc", 0), ("up", 0), ("gc", 2), ("gc", 1), ("up", 2), ("up", 1),
+    ("cnt", 0), ("hop", 0), ("cnt", 1), ("hop", 1), ("cnt", 2), ("zl", 0), ("fz",), ("zl", 1), ("mm", 1),
+    ("mm", 0), ("mm", 3), ("mm", 2), ("sx", 1), ("sx", 0), ("sx", 3), ("sz", 1), ("sx", 2), ("sz", 0),
+    ("sz", 3), ("fx",), ("gx", 1), ("sz", 2), ("gx", 0), ("gx", 3), ("turn", 1), ("gx", 2), ("turn", 0),
+    ("mm2", 0), ("turn", 3), ("turn", 2), ("mm2", 2), ("mm2", 1), ("sy", 0), ("sy", 2), ("adam", 0),
+    ("sy", 1), ("adam", 2), ("gy", 0), ("adam", 1), ("gy", 2), ("gy", 1), ("gc", 0), ("up", 0), ("gc", 2),
+    ("gc", 1), ("up", 2), ("up", 1),
 )
-N_SEM = 31 + 6 * N_PARTS
-N_FIXED = 21
-N_EACH = 9
+N_SEM = 34 + 5 * N_PARTS
+N_FIXED = 22
+N_EACH = 7
 
 
 def kernel(x_hbm, g_hbm, p_hbm, m_hbm, v_hbm, ids_ref, m_out, v_out, u_out, *scratch):
     (
         x_in, g_in, m_in, v_in, p_in, rows_in, rows_up,
         part32, part, x_got, xsum32, xsum, z_got, wide, wide_t,
-        count, count_got, u_sum,
+        count, count_got, ids_all, u_sum,
         loc_sem, send_sem, recv_sem,
     ) = scratch[:N_FIXED]
     of_part = [scratch[N_FIXED + N_EACH * e : N_FIXED + N_EACH * (e + 1)] for e in range(N_PARTS)]
@@ -84,8 +84,8 @@
 
     own_rows = pltpu.make_async_copy(p_hbm, p_in, loc_sem.at[0])
     loads = [
-        pltpu.make_async_copy(x_hbm, x_in, loc_sem.at[1]),
-        pltpu.make_async_copy(g_hbm, g_in, loc_sem.at[2]),
+        pltpu.make_async_copy(x_hbm, x_in.at[core], loc_sem.at[1]),
+        pltpu.make_async_copy(g_hbm, g_in.at[core], loc_sem.at[2]),
         pltpu.make_async_copy(m_hbm, m_in, loc_sem.at[3]),
         pltpu.make_async_copy(v_hbm, v_in, loc_sem.at[4]),
     ]
@@ -93,9 +93,9 @@
     for cp in loads:
         cp.start()
 
-    to_hop = device(y=up(zh, y), zl=x, zh=y, x=zl)
+    to_hop = [device(y=up(zh, y), zl=x, zh=y, x=zl, core=c) for c in range(2)]
     seat = up(y, 4 - zh)
-    from_hop = device(y=zh, zl=x, zh=seat, x=zl)
+    from_hop = [device(y=zh, zl=x, zh=seat, x=zl, core=c) for c in range(2)]
     moves = jnp.logical_or(x != zl, jnp.logical_or(y != 0, zh != 0))
     barrier = pltpu.get_barrier_semaphore()
     greet = [device(core=other)]
@@ -106,7 +106,8 @@
 
     @pl.when(moves)
     def _():
-        pl.semaphore_signal(barrier, inc=1, device_id=from_hop, device_id_type=MESH)
+        for to in from_hop:
+            pl.semaphore_signal(barrier, inc=1, device_id=to, device_id_type=MESH)
 
     own_rows.wait()
     held = p_in[...].astype(F32)
@@ -118,32 +119,54 @@
     moved = jnp.dot(turned, pick, preferred_element_type=F32).astype(BF)
     for r in range(4):
         h, c = divmod(r, 2)
-        rows_up[h, zh, x, :, c * QUARTER : (c + 1) * QUARTER] = moved[r * ROWS : (r + 1) * ROWS]
+        rows_up[h, c, zh, x] = moved[r * ROWS : (r + 1) * ROWS]
 
     ids = jnp.transpose(jnp.broadcast_to(ids_ref[...], (128, TOK)))
     match = (ids == lax.broadcasted_iota(jnp.int32, (TOK, 128), 1)).astype(F32)
     count[0] = jnp.broadcast_to(jnp.sum(match, axis=0, keepdims=True), (8, 128))
 
-    pl.semaphore_wait(barrier, len(greet) + moves.astype(jnp.int32))
-
-    def hop(h):
+    pl.semaphore_wait(barrier, len(greet) + 2 * moves.astype(jnp.int32))
+
+    def hop(h, c):
+        i = N_SEM - 1 - (2 * h + c)
         return pltpu.make_async_remote_copy(
-            src_ref=rows_up.at[h, zh, x], dst_ref=rows_in.at[h, core, zh, x],
-            send_sem=send_sem.at[N_SEM - 1 - h], recv_sem=recv_sem.at[N_SEM - 1 - h],
-            device_id=to_hop, device_id_type=MESH,
+            src_ref=rows_up.at[h, c, zh, x], dst_ref=rows_in.at[h, core, zh, x],
+            send_sem=send_sem.at[i], recv_sem=recv_sem.at[N_SEM - 1 - (2 * h + core)],
+            device_id=to_hop[c], device_id_type=MESH,
         )
+
+    def stay(h):
+        return pltpu.make_async_remote_copy(
+            src_ref=rows_up.at[h, other, zh, x], dst_ref=rows_in.at[h, core, zh, x],
+            send_sem=send_sem.at[N_SEM - 1 - (2 * h + other)],
+            recv_sem=recv_sem.at[N_SEM - 1 - (2 * h + core)],
+            device_id=device(core=other), device_id_type=MESH,
+        )
+
+    def hop_wait(h, c, sems):
+        whole = rows_up.at[h, c, zh, x]
+        pltpu.make_async_copy(whole, whole, sems.at[N_SEM - 1 - (2 * h + c)]).wait()
 
     @pl.when(moves)
     def _():
-        hop(0).start()
-        hop(1).start()
-
-    send(("CNT", 0), count_got.at[0], [(count.at[0], count_got.at[0], device(core=other))])
+        for h in range(2):
+            for c in range(2):
+                hop(h, c).start()
 
     @pl.when(jnp.logical_not(moves))
     def _():
         for h in range(2):
-            rows_in[h, core, zh, x] = rows_up[h, zh, x]
+            stay(h).start()
+            rows_in[h, core, zh, x] = rows_up[h, core, zh, x]
+
+    for cp in loads[:2]:
+        cp.wait()
+    to = device(core=other)
+    ids_all[core] = ids_ref[...]
+    send(("CNT", 0), count_got.at[0], [(count.at[0], count_got.at[0], to)])
+    send(("ids",), ids_all.at[0], [(ids_all.at[core], ids_all.at[core], to)])
+    send(("xin",), x_in.at[0], [(x_in.at[core], x_in.at[core], to)])
+    send(("gin",), g_in.at[0], [(g_in.at[core], g_in.at[core], to)])
 
     def do_cnt(i):
         if i == 0:
@@ -162,44 +185,43 @@
             arrive(("cnt", 1))
             lengths = count[2] + count_got[4] + count_got[5] + count_got[6]
             inverse = 1.0 / lengths[0:1]
-            mine = ids_ref[:, pl.ds(pl.multiple_of(x * 128, 128), 128)]
-            mine = jnp.transpose(jnp.broadcast_to(mine, (128, 128)))
-            here = mine == lax.broadcasted_iota(jnp.int32, (128, 128), 1)
-            weight = jnp.sum(jnp.where(here, inverse, 0.0), axis=1, keepdims=True)
-            weights[...] = jnp.broadcast_to(weight, (128, 128)).reshape(4, SUB, 128)
+            arrive(("ids",))
+            for b in range(2):
+                mine = ids_all[b, :, pl.ds(pl.multiple_of(x * 128, 128), 128)]
+                mine = jnp.transpose(jnp.broadcast_to(mine, (128, 128)))
+                here = mine == lax.broadcasted_iota(jnp.int32, (128, 128), 1)
+                weight = jnp.sum(jnp.where(here, inverse, 0.0), axis=1, keepdims=True)
+                weights[b] = jnp.broadcast_to(weight, (128, 128)).reshape(4, SUB, 128)
 
     def do_hop(h):
         @pl.when(moves)
         def _():
-            hop(h).wait_recv()
-
-        mine = rows_in.at[h, core, seat, zl]
-        send(("hop", h), rows_in.at[h, core, 0, pl.ds(0, 3)], [
+            for c in range(2):
+                hop_wait(h, c, recv_sem)
+
+        @pl.when(jnp.logical_not(moves))
+        def _():
+            hop_wait(h, other, recv_sem)
+
+        mine = rows_in.at[h, :, seat, zl]
+        send(("hop", h), rows_in.at[h, :, 0, pl.ds(0, 3)], [
             (mine, mine, device(zl=p)) for p in zl_peers
         ])
 
     def do_zl(h):
         arrive(("hop", h))
-        mine = rows_in.at[h, core, seat]
-        send(("zl", h), rows_in.at[h, core, pl.ds(0, 3)], [
+        mine = rows_in.at[h, :, seat]
+        send(("zl", h), rows_in.at[h, :, pl.ds(0, 3)], [
             (mine, mine, device(y=p)) for p in y_peers
         ])
 
-    def do_y(h):
-        arrive(("zl", h))
-        mine = rows_in.at[h, core]
-        send(("y", h), mine, [(mine, mine, device(core=other))])
-
     def do_mm(r):
-        h, c = divmod(r, 2)
-        if ("y", h) in flying:
-            arrive(("y", h))
-        if loads:
-            for cp in loads:
-                cp.wait()
-            loads.clear()
-        rhs = rows_in[h].reshape(FEAT, HALF)[:, c * QUARTER : (c + 1) * QUARTER]
-        value = jnp.dot(x_in[...], rhs, preferred_element_type=F32).reshape(4, 4, SUB, QUARTER)
+        h, b = divmod(r, 2)
+        for name in (("zl", h), ("xin",)):
+            if name in flying:
+                arrive(name)
+        rhs = rows_in[h].reshape(FEAT, QUARTER)
+        value = jnp.dot(x_in[b], rhs, preferred_element_type=F32).reshape(4, 4, SUB, QUARTER)
         part32[r] = value
         part[r] = value.astype(BF)
         send(("mm", r), x_got.at[r], [
@@ -222,7 +244,7 @@
         total = xsum32[r, zh]
         for k in range(3):
             total = total + z_got[r, k].astype(F32)
-        wide[r, x, zh] = (total * weights[zh][:, 0:1]).astype(BF)
+        wide[r, x, zh] = (total * weights[r % 2, zh][:, 0:1]).astype(BF)
         mine = wide.at[r, x, zh]
         send(("sz", r), wide.at[r, x, pl.ds(0, 3)], [(mine, mine, device(zh=p)) for p in zh_peers])
 
@@ -233,40 +255,38 @@
 
     def do_turn(r):
         arrive(("gx", r))
-        wide_t[r] = jnp.transpose(wide[r].reshape(TOK, QUARTER))
+        h, b = divmod(r, 2)
+        wide_t[h, :, b * TOK : (b + 1) * TOK] = jnp.transpose(wide[r].reshape(TOK, QUARTER))
 
     def do_fz():
-        mine = rows_up.at[:, zh, x]
-        send(("fz",), rows_up.at[:, pl.ds(0, 3), x], [(mine, mine, device(zh=p)) for p in zh_peers])
+        mine = rows_up.at[:, :, zh, x]
+        send(("fz",), rows_up.at[:, :, pl.ds(0, 3), x], [
+            (mine, mine, device(zh=p)) for p in zh_peers
+        ])
 
     def do_fx():
         arrive(("fz",))
-        mine = rows_up.at[:, :, x]
-        send(("fx",), rows_up.at[:, :, pl.ds(0, 3)], [(mine, mine, device(x=p)) for p in x_peers])
+        mine = rows_up.at[:, :, :, x]
+        send(("fx",), rows_up.at[:, :, :, pl.ds(0, 3)], [(mine, mine, device(x=p)) for p in x_peers])
 
     def do_mm2(e):
         h, start, width = PARTS[e]
-        g_own, g_peer, c_got = of_part[e][0:3]
-        cols = pl.ds(start, width)
-        value = jnp.dot(wide_t[2 * h + other], g_in[:, cols], preferred_element_type=F32)
-        g_peer[...] = value.astype(BF).reshape(4, 4, 16, width)
-        send(("mm2", e), c_got, [(g_peer, c_got, device(core=other))])
-        value = jnp.dot(wide_t[2 * h + core], g_in[:, cols], preferred_element_type=F32)
+        g_own, ysum, y_got = of_part[e][0:3]
+        if ("gin",) in flying:
+            arrive(("gin",))
+        rhs = g_in[...].reshape(2 * TOK, FF)[:, start : start + width]
+        value = jnp.dot(wide_t[h], rhs, preferred_element_type=F32)
         g_own[...] = value.reshape(4, 4, 16, width)
-
-    def do_sc(e):
-        g_own, _, c_got, ysum, y_got = of_part[e][0:5]
+        for k, p in enumerate(y_peers):
+            ysum[k] = g_own[p].astype(BF)
+        send(("mm2", e), y_got, [
+            (ysum.at[k], y_got.at[k], device(y=p)) for k, p in enumerate(y_peers)
+        ])
+
+    def do_sy(e):
+        g_own, _, y_got, zsum32, zsum, l_got = of_part[e][0:6]
+        total = g_own[y]
         arrive(("mm2", e))
-        for k, p in enumerate(y_peers):
-            ysum[k] = (g_own[p] + c_got[p].astype(F32)).astype(BF)
-        send(("sc", e), y_got, [
-            (ysum.at[k], y_got.at[k], device(y=p)) for k, p in enumerate(y_peers)
-        ])
-
-    def do_sy(e):
-        g_own, _, c_got, _, y_got, zsum32, zsum, l_got = of_part[e][0:8]
-        total = g_own[y] + c_got[y].astype(F32)
-        arrive(("sc", e))
         for k in range(3):
             total = total + y_got[k].astype(F32)
         zsum32[...] = total
@@ -277,12 +297,15 @@
 
     def do_adam(e):
         h, start, width = PARTS[e]
-        zsum32, _, l_got, full = of_part[e][5:9]
+        zsum32, _, l_got, full = of_part[e][3:7]
         rows, cols = pl.ds(h * 16, 16), pl.ds(start, width)
         arrive(("sy", e))
         grad = zsum32[zl]
         for k in range(3):
             grad = grad + l_got[k].astype(F32)
+        for cp in loads[2:]:
+            cp.wait()
+        del loads[2:]
         first = beta_first * m_in[rows, cols] + (1.0 - beta_first) * grad
         second = beta_second * v_in[rows, cols] + (1.0 - beta_second) * (grad * grad)
         way = first / bias_first / (jnp.sqrt(second / bias_second) + epsilon)
@@ -295,25 +318,31 @@
         v_new[rows, cols] = second
 
     def do_gy(e):
-        full = of_part[e][8]
+        full = of_part[e][6]
         arrive(("adam", e))
         mine = full.at[core, y]
         send(("gy", e), full.at[core, pl.ds(0, 3)], [(mine, mine, device(y=p)) for p in y_peers])
 
     def do_gc(e):
-        full = of_part[e][8]
+        full = of_part[e][6]
         arrive(("gy", e))
         mine = full.at[core]
         send(("gc", e), mine, [(mine, mine, device(core=other))])
 
     def do_up(e):
         h, start, width = PARTS[e]
-        full = of_part[e][8]
+        full = of_part[e][6]
         if ("fx",) in flying:
             arrive(("fx",))
+        value = jnp.dot(
+            rows_up[h, core].reshape(256, QUARTER), full[core].reshape(QUARTER, width),
+            preferred_element_type=F32,
+        )
         arrive(("gc", e))
-        lhs = rows_up[h].reshape(256, HALF)
-        value = jnp.dot(lhs, full[...].reshape(HALF, width), preferred_element_type=F32)
+        value = value + jnp.dot(
+            rows_up[h, other].reshape(256, QUARTER), full[other].reshape(QUARTER, width),
+            preferred_element_type=F32,
+        )
         if h == 0:
             u_sum[:, pl.ds(start, width)] = value
         else:
@@ -321,9 +350,9 @@
             u_new[:, pl.ds(start, width)] = value.astype(BF)
 
     steps = {
-        "hop": do_hop, "zl": do_zl, "y": do_y, "cnt": do_cnt, "mm": do_mm, "sx": do_sx,
+        "hop": do_hop, "zl": do_zl, "cnt": do_cnt, "mm": do_mm, "sx": do_sx,
         "sz": do_sz, "gx": do_gx, "turn": do_turn, "fz": do_fz, "fx": do_fx, "mm2": do_mm2,
-        "sc": do_sc, "sy": do_sy, "adam": do_adam, "gy": do_gy, "gc": do_gc, "up": do_up,
+        "sy": do_sy, "adam": do_adam, "gy": do_gy, "gc": do_gc, "up": do_up,
     }
     for name, *which in ORDER:
         steps[name](*which)
@@ -337,8 +366,14 @@
 
     @pl.when(moves)
     def _():
-        hop(0).wait_send()
-        hop(1).wait_send()
+        for h in range(2):
+            for c in range(2):
+                hop_wait(h, c, send_sem)
+
+    @pl.when(jnp.logical_not(moves))
+    def _():
+        for h in range(2):
+            hop_wait(h, other, send_sem)
 
     for whole, i in groups:
         pltpu.make_async_copy(whole, whole, send_sem.at[i]).wait()
@@ -361,13 +396,13 @@
 
 def local(layer_input, out_grad, projector, first_moment, second_moment, doc_ids):
     scratch = [
-        pltpu.VMEM((TOK, FEAT), BF),
-        pltpu.VMEM((TOK, FF), BF),
+        pltpu.VMEM((2, TOK, FEAT), BF),
+        pltpu.VMEM((2, TOK, FF), BF),
         pltpu.VMEM((MOM, FF), F32),
         pltpu.VMEM((MOM, FF), F32),
         pltpu.VMEM((ROWS, RANK), BF),
-        pltpu.VMEM((2, 2, 4, 4, ROWS, HALF), BF),
-        pltpu.VMEM((2, 4, 4, ROWS, HALF), BF),
+        pltpu.VMEM((2, 2, 4, 4, ROWS, QUARTER), BF),
+        pltpu.VMEM((2, 2, 4, 4, ROWS, QUARTER), BF),
         pltpu.VMEM((4, 4, 4, SUB, QUARTER), F32),
         pltpu.VMEM((4, 4, 4, SUB, QUARTER), BF),
         pltpu.VMEM((4, 3, 4, SUB, QUARTER), BF),
@@ -375,9 +410,10 @@
         pltpu.VMEM((4, 4, SUB, QUARTER), BF),
         pltpu.VMEM((4, 3, SUB, QUARTER), BF),
         pltpu.VMEM((4, 4, 4, SUB, QUARTER), BF),
-        pltpu.VMEM((4, QUARTER, TOK), BF),
+        pltpu.VMEM((2, QUARTER, 2 * TOK), BF),
         pltpu.VMEM((3, 8, 128), F32),
         pltpu.VMEM((7, 8, 128), F32),
+        pltpu.VMEM((2, 1, TOK), jnp.int32),
         pltpu.VMEM((256, FF), F32),
         pltpu.SemaphoreType.DMA((5,)),
         pltpu.SemaphoreType.DMA((N_SEM,)),
@@ -386,8 +422,6 @@
     for _, _, w in PARTS:
         scratch += [
             pltpu.VMEM((4, 4, 16, w), F32),
-            pltpu.VMEM((4, 4, 16, w), BF),
-            pltpu.VMEM((4, 4, 16, w), BF),
             pltpu.VMEM((3, 4, 16, w), BF),
             pltpu.VMEM((3, 4, 16, w), BF),
             pltpu.VMEM((4, 16, w), F32),
@@ -399,7 +433,7 @@
         pltpu.VMEM((MOM, FF), F32),
         pltpu.VMEM((MOM, FF), F32),
         pltpu.VMEM((256, FF), BF),
-        pltpu.VMEM((4, SUB, 128), F32),
+        pltpu.VMEM((2, 4, SUB, 128), F32),
     ]
     any_space = pl.BlockSpec(memory_space=pl.ANY)
     results = (

time: 110 us -> 105 us (0.955)
  Pallas kernels: 109 us -> 105 us
    pallas_call x1, Pallas kernels: 107 us -> 103 us  [local(): pl.pallas_call(kernel, out_shape=results, in_specs=[any_space] * 5 + [pl....]
where the time goes in v3:
time: 105 us
  Pallas kernels  105 us (100%)
    pallas_call x1, Pallas kernels, local(): pl.pallas_call(kernel, out_shape=results, in_specs=[any_space] * 5 + [pl....  103 us

profile of v3, /device:TPU:1, one launch (start us, length us, event | category | flops | bytes accessed | tf_op | source)
XLA Modules:
  0.0 105.2 jit_solution(7024487078646831704)
XLA Ops:
  0.6 102.6 %galore.1 = (f32[32,896]{1,0:T(8,128)}, f32[32,896]{1,0:T(8,128)}, bf16[256,896]{1,0:T(8,128)(2,1)}) custom-call(bf16[512,512]{1,0:T(8,128)(2,1)} %x_hbm.1, bf16[512,896]{1,0:T(8,128)(2,1)} %g_hbm.1, bf16[16,1024]{1,0:T(8,128)(2,1)} %p_hbm.1, f32[32,896]{1,0:T(8,128)} %m_hbm.1, f32[32,896]{1,0:T(8,128)} %v_hbm.1, s32[1,512]{1,0:T(1,128)} %bitcast.1), custom_call_target="tpu_custom_call" | custom-call | flops 2000000000 | bytes 4000000 | tf_op jit(solution)/shard_map/galore/pallas_call | solution.py:444
  103.3 2.0 %hand_on.1 = (f32[32,896]{1,0:T(8,128)}, f32[32,896]{1,0:T(8,128)}, bf16[256,896]{1,0:T(8,128)(2,1)}) custom-call(f32[32,896]{1,0:T(8,128)} %get-tuple-element.6.m_in, f32[32,896]{1,0:T(8,128)} %get-tuple-element.7.v_in, bf16[256,896]{1,0:T(8,128)(2,1)} %get-tuple-element.8.u_in), custom_call_target="tpu_custom_call" | custom-call | tf_op jit(solution)/shard_map/hand_on/pallas_call | solution.py:456

commit v4 on v3

--- a/solution.py
+++ b/solution.py
@@ -22,12 +22,12 @@
 PARTS = ((0, 0, 896), (1, 0, 384), (1, 384, 512))
 N_PARTS = len(PARTS)
 ORDER = (
-    ("cnt", 0), ("hop", 0), ("cnt", 1), ("hop", 1), ("cnt", 2), ("zl", 0), ("fz",), ("zl", 1), ("mm", 1),
-    ("mm", 0), ("mm", 3), ("mm", 2), ("sx", 1), ("sx", 0), ("sx", 3), ("sz", 1), ("sx", 2), ("sz", 0),
-    ("sz", 3), ("fx",), ("gx", 1), ("sz", 2), ("gx", 0), ("gx", 3), ("turn", 1), ("gx", 2), ("turn", 0),
-    ("mm2", 0), ("turn", 3), ("turn", 2), ("mm2", 2), ("mm2", 1), ("sy", 0), ("sy", 2), ("adam", 0),
-    ("sy", 1), ("adam", 2), ("gy", 0), ("adam", 1), ("gy", 2), ("gy", 1), ("gc", 0), ("up", 0), ("gc", 2),
-    ("gc", 1), ("up", 2), ("up", 1),
+    ("cnt", 0), ("hop", 0), ("cnt", 1), ("hop", 1), ("cnt", 2), ("zl", 0), ("zl", 1), ("mm", 1), ("mm", 0),
+    ("mm", 3), ("mm", 2), ("sx", 1), ("sx", 0), ("sx", 3), ("sz", 1), ("sx", 2), ("sz", 0), ("sz", 3),
+    ("gx", 1), ("sz", 2), ("gx", 0), ("gx", 3), ("turn", 1), ("gx", 2), ("fz",), ("turn", 0), ("mm2", 0),
+    ("turn", 3), ("turn", 2), ("mm2", 2), ("mm2", 1), ("fx",), ("sy", 0), ("sy", 2), ("adam", 0), ("sy", 1),
+    ("adam", 2), ("gy", 0), ("adam", 1), ("gy", 2), ("gy", 1), ("gc", 0), ("up", 0), ("gc", 2), ("gc", 1),
+    ("up", 2), ("up", 1),
 )
 N_SEM = 34 + 5 * N_PARTS
 N_FIXED = 22
@@ -58,10 +58,10 @@
         return lax.rem(value + k, 4)
 
     other = 1 - core
-    x_peers = [up(x, k) for k in (1, 3, 2)]
-    y_peers = [up(y, k) for k in (1, 3, 2)]
-    zl_peers = [up(zl, k) for k in (1, 3, 2)]
-    zh_peers = [up(zh, k) for k in (1, 3, 2)]
+    x_peers = [up(x, k) for k in (2, 1, 3)]
+    y_peers = [up(y, k) for k in (2, 1, 3)]
+    zl_peers = [up(zl, k) for k in (2, 1, 3)]
+    zh_peers = [up(zh, k) for k in (2, 1, 3)]
 
     used = [0]
     flying = {}

time: 105 us -> 103 us (0.981)
  Pallas kernels: 105 us -> 102 us
    pallas_call x1, Pallas kernels: 103 us -> 100 us  [local(): pl.pallas_call(kernel, out_shape=results, in_specs=[any_space] * 5 + [pl....]
where the time goes in v4:
time: 103 us
  Pallas kernels  102 us (99%)
    pallas_call x1, Pallas kernels, local(): pl.pallas_call(kernel, out_shape=results, in_specs=[any_space] * 5 + [pl....  100 us

profile of v4, /device:TPU:1, one launch (start us, length us, event | category | flops | bytes accessed | tf_op | source)
XLA Modules:
  0.0 102.8 jit_solution(7715655919763204497)
XLA Ops:
  0.6 100.2 %galore.1 = (f32[32,896]{1,0:T(8,128)}, f32[32,896]{1,0:T(8,128)}, bf16[256,896]{1,0:T(8,128)(2,1)}) custom-call(bf16[512,512]{1,0:T(8,128)(2,1)} %x_hbm.1, bf16[512,896]{1,0:T(8,128)(2,1)} %g_hbm.1, bf16[16,1024]{1,0:T(8,128)(2,1)} %p_hbm.1, f32[32,896]{1,0:T(8,128)} %m_hbm.1, f32[32,896]{1,0:T(8,128)} %v_hbm.1, s32[1,512]{1,0:T(1,128)} %bitcast.1), custom_call_target="tpu_custom_call" | custom-call | flops 2000000000 | bytes 4000000 | tf_op jit(solution)/shard_map/galore/pallas_call | solution.py:444
  100.8 2.0 %hand_on.1 = (f32[32,896]{1,0:T(8,128)}, f32[32,896]{1,0:T(8,128)}, bf16[256,896]{1,0:T(8,128)(2,1)}) custom-call(f32[32,896]{1,0:T(8,128)} %get-tuple-element.6.m_in, f32[32,896]{1,0:T(8,128)} %get-tuple-element.7.v_in, bf16[256,896]{1,0:T(8,128)(2,1)} %get-tuple-element.8.u_in), custom_call_target="tpu_custom_call" | custom-call | tf_op jit(solution)/shard_map/hand_on/pallas_call | solution.py:456

commit v5 on v4

--- a/solution.py
+++ b/solution.py
@@ -58,10 +58,10 @@
         return lax.rem(value + k, 4)
 
     other = 1 - core
-    x_peers = [up(x, k) for k in (2, 1, 3)]
-    y_peers = [up(y, k) for k in (2, 1, 3)]
-    zl_peers = [up(zl, k) for k in (2, 1, 3)]
-    zh_peers = [up(zh, k) for k in (2, 1, 3)]
+    x_peers = [up(x, k) for k in (2, 1 + 2 * core, 3 - 2 * core)]
+    y_peers = [up(y, k) for k in (2, 1 + 2 * core, 3 - 2 * core)]
+    zl_peers = [up(zl, k) for k in (2, 1 + 2 * core, 3 - 2 * core)]
+    zh_peers = [up(zh, k) for k in (2, 1 + 2 * core, 3 - 2 * core)]
 
     used = [0]
     flying = {}

time: 103 us -> 102 us (level)
  no operation moved by 1% of the time
where the time goes in v5:
time: 102 us
  Pallas kernels  102 us (100%)
    pallas_call x1, Pallas kernels, local(): pl.pallas_call(kernel, out_shape=results, in_specs=[any_space] * 5 + [pl....  99.6 us

profile of v5, /device:TPU:1, one launch (start us, length us, event | category | flops | bytes accessed | tf_op | source)
XLA Modules:
  0.0 102.2 jit_solution(14692067879282679099)
XLA Ops:
  0.6 99.6 %galore.1 = (f32[32,896]{1,0:T(8,128)}, f32[32,896]{1,0:T(8,128)}, bf16[256,896]{1,0:T(8,128)(2,1)}) custom-call(bf16[512,512]{1,0:T(8,128)(2,1)} %x_hbm.1, bf16[512,896]{1,0:T(8,128)(2,1)} %g_hbm.1, bf16[16,1024]{1,0:T(8,128)(2,1)} %p_hbm.1, f32[32,896]{1,0:T(8,128)} %m_hbm.1, f32[32,896]{1,0:T(8,128)} %v_hbm.1, s32[1,512]{1,0:T(1,128)} %bitcast.1), custom_call_target="tpu_custom_call" | custom-call | flops 2000000000 | bytes 4000000 | tf_op jit(solution)/shard_map/galore/pallas_call | solution.py:444
  100.3 2.0 %hand_on.1 = (f32[32,896]{1,0:T(8,128)}, f32[32,896]{1,0:T(8,128)}, bf16[256,896]{1,0:T(8,128)(2,1)}) custom-call(f32[32,896]{1,0:T(8,128)} %get-tuple-element.6.m_in, f32[32,896]{1,0:T(8,128)} %get-tuple-element.7.v_in, bf16[256,896]{1,0:T(8,128)(2,1)} %get-tuple-element.8.u_in), custom_call_target="tpu_custom_call" | custom-call | tf_op jit(solution)/shard_map/hand_on/pallas_call | solution.py:456

commit v6 on v5

--- a/solution.py
+++ b/solution.py
@@ -295,6 +295,12 @@
             (zsum.at[p], l_got.at[k], device(zl=p)) for k, p in enumerate(zl_peers)
         ])
 
+    stepped = []
+    outs = [
+        pltpu.make_async_copy(value, out, loc_sem.at[i])
+        for i, (value, out) in enumerate(((m_new, m_out), (v_new, v_out)))
+    ]
+
     def do_adam(e):
         h, start, width = PARTS[e]
         zsum32, _, l_got, full = of_part[e][3:7]
@@ -316,6 +322,10 @@
         ])
         m_new[rows, cols] = first
         v_new[rows, cols] = second
+        stepped.append(e)
+        if len(stepped) == N_PARTS:
+            for cp in outs[:2]:
+                cp.start()
 
     def do_gy(e):
         full = of_part[e][6]
@@ -348,6 +358,10 @@
         else:
             value = value + u_sum[:, pl.ds(start, width)]
             u_new[:, pl.ds(start, width)] = value.astype(BF)
+            cols = pl.ds(start, width)
+            cp = pltpu.make_async_copy(u_new.at[:, cols], u_out.at[:, cols], loc_sem.at[len(outs)])
+            cp.start()
+            outs.append(cp)
 
     steps = {
         "hop": do_hop, "zl": do_zl, "cnt": do_cnt, "mm": do_mm, "sx": do_sx,
@@ -356,13 +370,6 @@
     }
     for name, *which in ORDER:
         steps[name](*which)
-
-    outs = [
-        pltpu.make_async_copy(value, out, loc_sem.at[i])
-        for i, (value, out) in enumerate(((m_new, m_out), (v_new, v_out), (u_new, u_out)))
-    ]
-    for cp in outs:
-        cp.start()
 
     @pl.when(moves)
     def _():

time: 102 us -> 102 us (level)
  no operation moved by 1% of the time
where the time goes in v6:
time: 102 us
  Pallas kernels  102 us (100%)
    pallas_call x1, Pallas kernels, local(): pl.pallas_call(kernel, out_shape=results, in_specs=[any_space] * 5 + [pl....  99.6 us

profile of v6, /device:TPU:1, one launch (start us, length us, event | category | flops | bytes accessed | tf_op | source)
XLA Modules:
  0.0 102.2 jit_solution(12232272669271547614)
XLA Ops:
  0.6 99.6 %galore.1 = (f32[32,896]{1,0:T(8,128)}, f32[32,896]{1,0:T(8,128)}, bf16[256,896]{1,0:T(8,128)(2,1)}) custom-call(bf16[512,512]{1,0:T(8,128)(2,1)} %x_hbm.1, bf16[512,896]{1,0:T(8,128)(2,1)} %g_hbm.1, bf16[16,1024]{1,0:T(8,128)(2,1)} %p_hbm.1, f32[32,896]{1,0:T(8,128)} %m_hbm.1, f32[32,896]{1,0:T(8,128)} %v_hbm.1, s32[1,512]{1,0:T(1,128)} %bitcast.1), custom_call_target="tpu_custom_call" | custom-call | flops 2000000000 | bytes 4000000 | tf_op jit(solution)/shard_map/galore/pallas_call | solution.py:451
  100.2 2.0 %hand_on.1 = (f32[32,896]{1,0:T(8,128)}, f32[32,896]{1,0:T(8,128)}, bf16[256,896]{1,0:T(8,128)(2,1)}) custom-call(f32[32,896]{1,0:T(8,128)} %get-tuple-element.6.m_in, f32[32,896]{1,0:T(8,128)} %get-tuple-element.7.v_in, bf16[256,896]{1,0:T(8,128)(2,1)} %get-tuple-element.8.u_in), custom_call_target="tpu_custom_call" | custom-call | tf_op jit(solution)/shard_map/hand_on/pallas_call | solution.py:463
